TPU v7x, 32 devices: a whole 2x2x4 slice. The times are simulated.
32 devices in a mesh: view: 2 (over x), band: 4 (over z), batch: 4 (over y, core).
Axes of the slice: x: 2, y: 2, z: 4, core: 2. Of those that a mesh axis runs over, the one named last changes fastest.
Arguments:
- images: bfloat16 [8, 32, 16, 768], P(('batch', 'view'), 'band'), parts along dimension 0, may hold values from -6 to 6
- frame_gain: float32 [768], replicated, may hold values from 0.5 to 2.5
- frame_qkv: bfloat16 [768, 1536], replicated, may hold values from -0.3 to 0.3
- frame_out: bfloat16 [512, 768], replicated, may hold values from -0.25 to 0.25
- row1_gain: float32 [768], replicated, may hold values from 0.5 to 2.5
- row1_qkv: bfloat16 [768, 1536], P('band'), may hold values from -0.3 to 0.3
- row1_out: bfloat16 [512, 768], P(None, 'band'), may hold values from -0.25 to 0.25
- row2_gain: float32 [768], replicated, may hold values from 0.5 to 2.5
- row2_qkv: bfloat16 [768, 1536], P('band'), may hold values from -0.3 to 0.3
- row2_out: bfloat16 [512, 768], P(None, 'band'), may hold values from -0.25 to 0.25
Outputs:
- refined: bfloat16 [8, 32, 16, 768], P(('batch', 'view'), 'band'), parts along dimension 0
There are 4 independent parts, one for each index of `batch`. A program takes and returns all parts, laid end to end along the dimension named above; an argument that names none is the same for every part. Nothing has to cross between parts.
All inputs are finite; a program needn't handle non-finite values.
Results may differ from a plain program's by a relative error of at most 0.02.
Values may be sent and summed in bfloat16 or wider, within the bound.
A program may use at most 64 MiB of HBM per device.

v0:
```python
import jax
import jax.numpy as jnp
from jax import lax
from jax.sharding import PartitionSpec as P

HEAD_DIM = 64


EPSILON = 1e-06
BLOCK_ROWS = 512


def rms_normed(stream, gain):
    values = stream.astype(jnp.float32)
    factor = lax.rsqrt(jnp.mean(values * values, axis=-1, keepdims=True) + EPSILON)
    return (values * factor * gain).astype(jnp.bfloat16)


def online_update(carry, queries, keys, values):
    running, total, accum = carry
    scores = jnp.einsum(
        "qhd,khd->hqk", queries, keys, preferred_element_type=jnp.float32
    ) * HEAD_DIM ** (-0.5)
    highest = jnp.maximum(running, jnp.max(scores, axis=-1))
    weights = jnp.exp(scores - highest[:, :, None])
    total = jnp.sum(weights, axis=-1)
    mixed = jnp.einsum(
        "hqk,khd->qhd", weights.astype(jnp.bfloat16), values, preferred_element_type=jnp.float32
    )
    accum = mixed
    return (highest, total, accum)


def unit_attention(trio):
    queries, keys, values = trio
    length, pair_width = queries.shape
    block = min(BLOCK_ROWS, length)
    keys = keys.reshape(length, 2, HEAD_DIM)
    values = values.reshape(length, 2, HEAD_DIM)
    blocks = queries.reshape(length // block, block, 2, HEAD_DIM)

    def one_block(query_block):
        scores = jnp.einsum(
            "qhd,khd->hqk", query_block, keys, preferred_element_type=jnp.float32
        ) * HEAD_DIM ** (-0.5)
        weights = jnp.exp(scores - jnp.max(scores, axis=-1, keepdims=True))
        mixed = jnp.einsum(
            "hqk,khd->qhd", weights.astype(jnp.bfloat16), values, preferred_element_type=jnp.float32
        )
        total = jnp.transpose(jnp.sum(weights, axis=-1))
        return (mixed / total[:, :, None]).astype(jnp.bfloat16).reshape(block, pair_width)

    return lax.map(one_block, blocks).reshape(length, pair_width)


def attend_units(pieces):
    queries, keys, values = pieces
    attended = lax.map(unit_attention, (queries[0], keys[0], values[0]))
    return lax.all_to_all(attended[None], "view", split_axis=2, concat_axis=0, tiled=True)


def project_parts(normed, shard):
    groups = shard.shape[1] // (2 * HEAD_DIM)
    piece = lax.all_gather(shard, "band", axis=0, tiled=True)
    count = piece.shape[0]
    return jnp.einsum(
        "rcd,dpw->rpcw",
        normed,
        piece.reshape(count, groups, 2 * HEAD_DIM),
        preferred_element_type=jnp.float32,
    )


def mix_parts(merged, shard):
    groups = merged.shape[1]
    piece = lax.all_gather(shard, "band", axis=1, tiled=True)
    count = piece.shape[1]
    return jnp.einsum(
        "rpcw,pwn->rcn",
        merged,
        piece.reshape(groups, 2 * HEAD_DIM, count),
        preferred_element_type=jnp.float32,
    )


def row_sublayer(stream, row_count, col_count, gain, project, mix):
    width = stream.shape[1]
    normed = rms_normed(stream, gain).reshape(row_count, col_count, width)
    projected = project(normed)
    groups = projected.shape[1] // 3
    views = lax.axis_size("view")

    def unit_layout(section):
        return section.astype(jnp.bfloat16).reshape(
            views, row_count * groups // views, col_count, 2 * HEAD_DIM
        )

    triple = (
        unit_layout(projected[:, :groups]),
        unit_layout(projected[:, groups : 2 * groups]),
        unit_layout(projected[:, 2 * groups :]),
    )
    returned = attend_units(
        (
            lax.all_to_all(triple[0], "view", split_axis=0, concat_axis=2, tiled=True),
            lax.all_to_all(triple[1], "view", split_axis=0, concat_axis=2, tiled=True),
            lax.all_to_all(triple[2], "view", split_axis=0, concat_axis=2, tiled=True),
        )
    )
    merged = returned.reshape(row_count, groups, col_count, 2 * HEAD_DIM)
    update = mix(merged).reshape(row_count * col_count, width)
    return (stream.astype(jnp.float32) + update).astype(jnp.bfloat16)


def local(
    images,
    frame_gain,
    frame_qkv,
    frame_out,
    row1_gain,
    row1_qkv,
    row1_out,
    row2_gain,
    row2_qkv,
    row2_out,
):
    _, row_count, col_count, width = images.shape
    inner = frame_out.shape[0]
    heads = inner // HEAD_DIM
    tokens = row_count * col_count
    stream = images.reshape(tokens, width)
    normed = rms_normed(stream, frame_gain)
    start_state = (
        jnp.full((heads, tokens), -1e30, jnp.float32),
        jnp.zeros((heads, tokens), jnp.float32),
        jnp.zeros((tokens, heads, HEAD_DIM), jnp.float32),
    )
    queries = (
        jnp.dot(normed, frame_qkv[:, :inner], preferred_element_type=jnp.float32)
        .astype(jnp.bfloat16)
        .reshape(tokens, heads, HEAD_DIM)
    )
    piece = lax.all_gather(normed, "band", axis=0, tiled=True)
    count = piece.shape[0]
    paired = jnp.dot(piece, frame_qkv[:, inner:], preferred_element_type=jnp.float32).astype(
        jnp.bfloat16
    )
    result = online_update(
        start_state,
        queries,
        paired[:, :inner].reshape(count, heads, HEAD_DIM),
        paired[:, inner:].reshape(count, heads, HEAD_DIM),
    )
    _, total, accum = result
    attended = (
        (accum / jnp.transpose(total)[:, :, None]).astype(jnp.bfloat16).reshape(tokens, inner)
    )
    update = jnp.dot(attended, frame_out, preferred_element_type=jnp.float32)
    stream = (stream.astype(jnp.float32) + update).astype(jnp.bfloat16)
    stream = row_sublayer(
        stream,
        row_count,
        col_count,
        row1_gain,
        lambda normed_rows: project_parts(normed_rows, row1_qkv),
        lambda merged: mix_parts(merged, row1_out),
    )
    stream = row_sublayer(
        stream,
        row_count,
        col_count,
        row2_gain,
        lambda normed_rows: project_parts(normed_rows, row2_qkv),
        lambda merged: mix_parts(merged, row2_out),
    )
    return stream.reshape(images.shape)


def solution(mesh):
    in_specs = (
        P(("batch", "view"), "band", None, None),
        P(),
        P(),
        P(),
        P(),
        P("band", None),
        P(None, "band"),
        P(),
        P("band", None),
        P(None, "band"),
    )
    out_specs = P(("batch", "view"), "band", None, None)
    return jax.shard_map(local, mesh=mesh, in_specs=in_specs, out_specs=out_specs, check_vma=False)
```

profile of v0, /device:TPU:0, one launch (start us, length us, event | category | flops | bytes accessed | tf_op | source)
XLA Modules:
  0.0 226.7 jit_solution(6524348358339169571)
XLA Ops:
  6.5 0.7 all-gather.3.cloned.1.call-update
  7.3 1.0 multiply_reduce_fusion.3
  8.4 1.0 fusion.41
  9.4 27.2 %all_gather.15 = bf16[512,768]{1,0:T(8,128)(2,1)S(1)} all-gather(bf16[128,768]{1,0:T(8,128)(2,1)S(1)} %fusion.41), channel_id=1, replica_groups=mesh['view'=2,'band'=4,'batch'=4] {'band'}, dimensions={0}, use_global_device_ids=true | all-gather | bytes 983040 | tf_op jit(solution)/shard_map/all_gather | solution.py:143
  36.7 2.4 %fusion.22 = bf16[512,1024]{1,0:T(8,128)(2,1)S(1)} fusion(bf16[512,768]{1,0:T(8,128)(2,1)S(1)} %all_gather.15, bf16[768,1536]{1,0:T(8,128)(2,1)} %param.16), kind=kOutput, calls=%fused_computation.36 | convolution fusion | flops 805830656 | bytes 3407872 | tf_op jit(solution)/shard_map/dot_general | solution.py:145
  39.1 0.2 copy.92
  39.4 1.4 convolution_convert_fusion.2
  40.9 0.2 copy.90
  41.1 0.6 multiply_reduce_fusion
  41.7 0.6 fusion.18
  42.3 0.6 fusion.35
  42.9 0.3 copy-done.3
  43.2 0.4 multiply_reduce_fusion.2
  43.6 0.8 multiply_convert_fusion.1
  44.4 23.0 %all-gather.3.cloned.1.call-done = bf16[768,1536]{1,0:T(8,128)(2,1)} async-done(((bf16[192,1536]{1,0:T(8,128)(2,1)}), bf16[768,1536]{1,0:T(8,128)(2,1)}) %all-gather.3.cloned.1.call-update) | async-done | bytes 2359312 | tf_op jit(solution)/shard_map/all_gather | solution.py:64
  67.3 2.8 %copy.93 = bf16[768,1536]{0,1:T(8,128)(2,1)S(1)} copy(bf16[768,1536]{1,0:T(8,128)(2,1)} %all-gather.3.cloned.1.call-done) | data formatting | bytes 4718592 | tf_op jit(solution)/shard_map/all_gather | solution.py:64
  70.2 1.8 fusion.25
  72.0 0.7 fusion.47
  72.7 7.0 %all_to_all.120 = bf16[2,16,16,128]{3,2,1,0:T(8,128)(2,1)S(1)} all-to-all(bf16[2,16,16,128]{3,2,1,0:T(8,128)(2,1)S(1)} %bitcast.165), channel_id=1, replica_groups=mesh['view'=2,'band'=4,'batch'=4] {'view'}, dimensions={0} | all-to-all | bytes 262144 | tf_op jit(solution)/shard_map/all_to_all | solution.py:107
  79.7 6.8 %all_to_all.121 = bf16[2,16,16,128]{3,2,1,0:T(8,128)(2,1)S(1)} all-to-all(bf16[2,16,16,128]{3,2,1,0:T(8,128)(2,1)S(1)} %bitcast.163), channel_id=1, replica_groups=mesh['view'=2,'band'=4,'batch'=4] {'view'}, dimensions={0} | all-to-all | bytes 262144 | tf_op jit(solution)/shard_map/all_to_all | solution.py:105
  86.5 3.4 %all-to-all-start.2 = ((bf16[2,16,16,128]{3,2,1,0:T(8,128)(2,1)}), bf16[2,16,16,128]{3,2,1,0:T(8,128)(2,1)S(1)}, u32[]{:S(2)}, u32[]{:S(2)}) async-start(bf16[2,16,16,128]{3,2,1,0:T(8,128)(2,1)} %bitcast.25), calls=%async_computation.2 | async-start | bytes 262144 | tf_op jit(solution)/shard_map/all_to_all | solution.py:106
  90.0 0.7 all-gather.5.cloned.1.call-update
  90.7 3.7 %all-to-all-done.2 = bf16[2,16,16,128]{3,2,1,0:T(8,128)(2,1)S(1)} async-done(((bf16[2,16,16,128]{3,2,1,0:T(8,128)(2,1)}), bf16[2,16,16,128]{3,2,1,0:T(8,128)(2,1)S(1)}, u32[]{:S(2)}, u32[]{:S(2)}) %all-to-all-start.2) | async-done | bytes 131104 | tf_op jit(solution)/shard_map/all_to_all | solution.py:106
  94.4 12.5 %while.20 = (s32[]{:T(128)}, bf16[16,32,128]{2,1,0:T(8,128)(2,1)S(1)}, bf16[16,32,128]{2,1,0:T(8,128)(2,1)S(1)}, bf16[16,32,128]{2,1,0:T(8,128)(2,1)S(1)}, bf16[16,32,128]{2,1,0:T(8,128)(2,1)S(1)}, /*index=5*/s32[]{:T(128)}) while((s32[]{:T(128)}, bf16[16,32,128]{2,1,0:T(8,128)(2,1)S(1)}, bf16[16,32,128]{2,1,0:T(8,128)(2,1)S(1)}, ...), condition=%wide.region_7.0_spmd, body=%wide.region_4.7_spmd.sunk | while | flops 544642 | bytes 206161 | solution.py:58
  94.9 0.2 fusion.77
  95.7 0.2 fusion.77
  97.2 0.2 fusion.77
  106.9 0.7 copy.144
  107.6 4.0 %all-to-all-start.3 = ((bf16[1,16,32,128]{3,1,0,2:T(8,128)(2,1)}), bf16[1,16,32,128]{3,1,0,2:T(8,128)(2,1)}, u32[]{:S(2)}, u32[]{:S(2)}) async-start(bf16[1,16,32,128]{3,1,0,2:T(8,128)(2,1)} %bitcast.133), calls=%async_computation.3 | async-start | bytes 262144 | tf_op jit(solution)/shard_map/all_to_all | solution.py:59
  111.7 29.0 %all_gather.17 = bf16[512,768]{0,1:T(8,128)(2,1)S(1)} all-gather(bf16[512,192]{0,1:T(8,128)(2,1)S(1)} %copy-done.4), channel_id=1, replica_groups=mesh['view'=2,'band'=4,'batch'=4] {'band'}, dimensions={1}, use_global_device_ids=true | all-gather | bytes 983040 | tf_op jit(solution)/shard_map/all_gather | solution.py:76
  140.6 1.2 copy.102
  141.8 14.2 %all-gather.5.cloned.1.call-done = bf16[768,1536]{1,0:T(8,128)(2,1)} async-done(((bf16[192,1536]{1,0:T(8,128)(2,1)}), bf16[768,1536]{1,0:T(8,128)(2,1)}) %all-gather.5.cloned.1.call-update) | async-done | bytes 2359312 | tf_op jit(solution)/shard_map/all_gather | solution.py:64
  156.0 2.8 %copy.103 = bf16[768,1536]{0,1:T(8,128)(2,1)S(1)} copy(bf16[768,1536]{1,0:T(8,128)(2,1)} %all-gather.5.cloned.1.call-done) | data formatting | bytes 4718592 | tf_op jit(solution)/shard_map/all_gather | solution.py:64
  158.9 0.9 copy.99
  159.8 1.5 multiply_reduce_fusion.1
  161.4 0.7 copy-done.1
  162.2 0.9 fusion.26
  163.1 0.7 fusion.46
  163.8 6.8 %all_to_all.122 = bf16[2,16,16,128]{3,2,1,0:T(8,128)(2,1)S(1)} all-to-all(bf16[2,16,16,128]{3,2,1,0:T(8,128)(2,1)S(1)} %bitcast.166), channel_id=1, replica_groups=mesh['view'=2,'band'=4,'batch'=4] {'view'}, dimensions={0} | all-to-all | bytes 262144 | tf_op jit(solution)/shard_map/all_to_all | solution.py:107
  170.6 6.8 %all_to_all.123 = bf16[2,16,16,128]{3,2,1,0:T(8,128)(2,1)S(1)} all-to-all(bf16[2,16,16,128]{3,2,1,0:T(8,128)(2,1)S(1)} %bitcast.164), channel_id=1, replica_groups=mesh['view'=2,'band'=4,'batch'=4] {'view'}, dimensions={0} | all-to-all | bytes 262144 | tf_op jit(solution)/shard_map/all_to_all | solution.py:105
  177.5 3.5 %all-to-all-start.6 = ((bf16[2,16,16,128]{3,2,1,0:T(8,128)(2,1)}), bf16[2,16,16,128]{3,2,1,0:T(8,128)(2,1)S(1)}, u32[]{:S(2)}, u32[]{:S(2)}) async-start(bf16[2,16,16,128]{3,2,1,0:T(8,128)(2,1)} %bitcast.51), calls=%async_computation.6 | async-start | bytes 262144 | tf_op jit(solution)/shard_map/all_to_all | solution.py:106
  181.0 4.4 %all-to-all-done.6 = bf16[2,16,16,128]{3,2,1,0:T(8,128)(2,1)S(1)} async-done(((bf16[2,16,16,128]{3,2,1,0:T(8,128)(2,1)}), bf16[2,16,16,128]{3,2,1,0:T(8,128)(2,1)S(1)}, u32[]{:S(2)}, u32[]{:S(2)}) %all-to-all-start.6) | async-done | bytes 131104 | tf_op jit(solution)/shard_map/all_to_all | solution.py:106
  185.5 12.5 %while.21 = (s32[]{:T(128)}, bf16[16,32,128]{2,1,0:T(8,128)(2,1)S(1)}, bf16[16,32,128]{2,1,0:T(8,128)(2,1)S(1)}, bf16[16,32,128]{2,1,0:T(8,128)(2,1)S(1)}, bf16[16,32,128]{2,1,0:T(8,128)(2,1)S(1)}, /*index=5*/s32[]{:T(128)}) while((s32[]{:T(128)}, bf16[16,32,128]{2,1,0:T(8,128)(2,1)S(1)}, bf16[16,32,128]{2,1,0:T(8,128)(2,1)S(1)}, ...), condition=%wide.region_12.13_spmd, body=%wide.region_9.12_spmd.sunk | while | flops 544642 | bytes 206161 | solution.py:58
  198.0 0.7 copy.143
  198.7 3.4 %all-to-all-start.7 = ((bf16[1,16,32,128]{3,1,0,2:T(8,128)(2,1)}), bf16[1,16,32,128]{3,1,0,2:T(8,128)(2,1)S(1)}, u32[]{:S(2)}, u32[]{:S(2)}) async-start(bf16[1,16,32,128]{3,1,0,2:T(8,128)(2,1)} %bitcast.132), calls=%async_computation.7 | async-start | bytes 262144 | tf_op jit(solution)/shard_map/all_to_all | solution.py:59
  202.1 16.5 %all_gather.19 = bf16[512,768]{0,1:T(8,128)(2,1)S(1)} all-gather(bf16[512,192]{0,1:T(8,128)(2,1)S(1)} %copy-done.5), channel_id=1, replica_groups=mesh['view'=2,'band'=4,'batch'=4] {'band'}, dimensions={1}, use_global_device_ids=true | all-gather | bytes 983040 | tf_op jit(solution)/shard_map/all_gather | solution.py:76
  218.5 0.3 copy.112
  218.9 1.0 fusion.29
  (388 shorter events, 24.2 us)
Async XLA Ops:
  6.5 36.4 %copy-start = (bf16[512,768]{1,0:T(8,128)(2,1)S(1)}, bf16[512,768]{1,0:T(8,128)(2,1)}, u32[]{:S(2)}) copy-start(bf16[512,768]{1,0:T(8,128)(2,1)} %param.17) | copy-start | bytes 2359300
  6.5 60.8 %all-gather.3.cloned.1.call-start = ((), (), s32[]{:S(2)}) async-start(), calls=%async_computation.8 | async-start | bytes 2949120 | tf_op jit(solution)/shard_map/all_gather | solution.py:64
  42.3 0.9 copy-start.3
  42.3 1.3 copy-start.6
  86.5 7.8 %all-to-all-start.2 = ((bf16[2,16,16,128]{3,2,1,0:T(8,128)(2,1)}), bf16[2,16,16,128]{3,2,1,0:T(8,128)(2,1)S(1)}, u32[]{:S(2)}, u32[]{:S(2)}) async-start(bf16[2,16,16,128]{3,2,1,0:T(8,128)(2,1)} %bitcast.25), calls=%async_computation.2 | async-start | bytes 262144 | tf_op jit(solution)/shard_map/all_to_all | solution.py:106
  89.9 66.1 %all-gather.5.cloned.1.call-start = ((), (), s32[]{:S(2)}) async-start(), calls=%async_computation.9 | async-start | bytes 2949120 | tf_op jit(solution)/shard_map/all_gather | solution.py:64
  90.7 21.0 %copy-start.4 = (bf16[512,192]{0,1:T(8,128)(2,1)S(1)}, bf16[512,192]{0,1:T(8,128)(2,1)}, u32[]{:S(2)}) copy-start(bf16[512,192]{0,1:T(8,128)(2,1)} %param.20) | copy-start | bytes 589828
  107.6 51.2 %all-to-all-start.3 = ((bf16[1,16,32,128]{3,1,0,2:T(8,128)(2,1)}), bf16[1,16,32,128]{3,1,0,2:T(8,128)(2,1)}, u32[]{:S(2)}, u32[]{:S(2)}) async-start(bf16[1,16,32,128]{3,1,0,2:T(8,128)(2,1)} %bitcast.133), calls=%async_computation.3 | async-start | bytes 262144 | tf_op jit(solution)/shard_map/all_to_all | solution.py:59
  158.8 3.3 %copy-start.7 = (f32[768]{0:T(1024)S(1)}, f32[768]{0:T(1024)}, u32[]{:S(2)}) copy-start(f32[768]{0:T(1024)} %param.21) | copy-start | bytes 9220
  161.3 0.8 copy-start.1
  177.5 24.6 %copy-start.5 = (bf16[512,192]{0,1:T(8,128)(2,1)S(1)}, bf16[512,192]{0,1:T(8,128)(2,1)}, u32[]{:S(2)}) copy-start(bf16[512,192]{0,1:T(8,128)(2,1)} %param.23) | copy-start | bytes 589828
  177.5 8.0 %all-to-all-start.6 = ((bf16[2,16,16,128]{3,2,1,0:T(8,128)(2,1)}), bf16[2,16,16,128]{3,2,1,0:T(8,128)(2,1)S(1)}, u32[]{:S(2)}, u32[]{:S(2)}) async-start(bf16[2,16,16,128]{3,2,1,0:T(8,128)(2,1)} %bitcast.51), calls=%async_computation.6 | async-start | bytes 262144 | tf_op jit(solution)/shard_map/all_to_all | solution.py:106
  198.0 20.9 %copy-start.2 = (f32[128,768]{1,0:T(8,128)S(1)}, f32[128,768]{1,0:T(8,128)}, u32[]{:S(2)}) copy-start(f32[128,768]{1,0:T(8,128)} %copy-done.1) | copy-start | bytes 1179652
  198.7 20.1 %all-to-all-start.7 = ((bf16[1,16,32,128]{3,1,0,2:T(8,128)(2,1)}), bf16[1,16,32,128]{3,1,0,2:T(8,128)(2,1)S(1)}, u32[]{:S(2)}, u32[]{:S(2)}) async-start(bf16[1,16,32,128]{3,1,0,2:T(8,128)(2,1)} %bitcast.132), calls=%async_computation.7 | async-start | bytes 262144 | tf_op jit(solution)/shard_map/all_to_all | solution.py:59
Sparse Core Ops, SparseCore 0:
  8.9 58.3 all-gather.2
  92.3 63.6 all-gather.4
where the time goes:
time: 228 us; the launch traced here: 227 us
  blocking collectives  100 us (44%)
  waiting for transfers between devices  46.6 us (20%)
  local copies, waits for them, and re-layouts  24.8 us (11%)
  matrix products  21.6 us (9%)
  starting transfers between devices  14.3 us (6%)
  between operations  13.8 us (6%)
  other arithmetic  4.57 us (2%)
    all_gather x2, blocking collectives, mix_parts(): piece = lax.all_gather(shard, 'band', axis=1, tiled=True)  45.4 us
    all_gather x2, waiting for transfers between devices, project_parts(): piece = lax.all_gather(shard, 'band', axis=0, tiled=True)  37.2 us
    all_gather x1, blocking collectives, local(): piece = lax.all_gather(normed, 'band', axis=0, tiled=True)  27.2 us
    all_to_all x2, blocking collectives, row_sublayer(): lax.all_to_all(triple[2], 'view', split_axis=0, concat_axis=2, tiled=True)  13.9 us
    all_to_all x2, blocking collectives, row_sublayer(): lax.all_to_all(triple[0], 'view', split_axis=0, concat_axis=2, tiled=True)  13.7 us
    all_to_all x2, waiting for transfers between devices, row_sublayer(): lax.all_to_all(triple[1], 'view', split_axis=0, concat_axis=2, tiled=True)  8.08 us
    all_to_all x2, starting transfers between devices, attend_units(): lax.all_to_all(attended[None], 'view', split_axis=2, concat_axis=0, tiled...  7.38 us
    all_to_all x2, starting transfers between devices, row_sublayer(): lax.all_to_all(triple[1], 'view', split_axis=0, concat_axis=2, tiled=True)  6.89 us
  transfers between devices with their start and end apart: 6, of which 4 were waited for; matrix products, arithmetic and copies ran while one was open for 12% of the time, Pallas kernels for 0%

commit v1 on v0

--- a/solution.py
+++ b/solution.py
@@ -1,6 +1,10 @@
+import functools
+
 import jax
 import jax.numpy as jnp
 from jax import lax
+from jax.experimental import pallas as pl
+from jax.experimental.pallas import tpu as pltpu
 from jax.sharding import PartitionSpec as P
 
 HEAD_DIM = 64
@@ -110,6 +114,128 @@
     merged = returned.reshape(row_count, groups, col_count, 2 * HEAD_DIM)
     update = mix(merged).reshape(row_count * col_count, width)
     return (stream.astype(jnp.float32) + update).astype(jnp.bfloat16)
+
+
+def attend_pair(queries, keys, values, mask):
+    lane = lax.broadcasted_iota(jnp.int32, queries.shape, 1)
+    sides = []
+    for side in range(2):
+        own = (lane >= side * HEAD_DIM) & (lane < (side + 1) * HEAD_DIM)
+        scores = lax.dot_general(
+            jnp.where(own, queries, jnp.zeros_like(queries)),
+            keys,
+            (((1,), (1,)), ((), ())),
+            preferred_element_type=jnp.float32,
+        ) * HEAD_DIM ** (-0.5)
+        if mask is not None:
+            scores = jnp.where(mask, scores, -jnp.inf)
+        weights = jnp.exp(scores - jnp.max(scores, axis=-1, keepdims=True))
+        total = jnp.sum(weights, axis=-1, keepdims=True)
+        mixed = jnp.dot(weights.astype(jnp.bfloat16), values, preferred_element_type=jnp.float32)
+        sides.append(mixed / total)
+    return jnp.where(lane < HEAD_DIM, sides[0], sides[1]).astype(jnp.bfloat16)
+
+
+def row_layer(stream, gain, weights, inner, mask):
+    pair = 2 * HEAD_DIM
+    normed = rms_normed(stream, gain)
+    projected = jnp.dot(normed, weights[:, : 3 * inner], preferred_element_type=jnp.float32)
+    projected = projected.astype(jnp.bfloat16)
+    parts = []
+    for at in range(0, inner, pair):
+        parts.append(
+            attend_pair(
+                projected[:, at : at + pair],
+                projected[:, inner + at : inner + at + pair],
+                projected[:, 2 * inner + at : 2 * inner + at + pair],
+                mask,
+            )
+        )
+    attended = jnp.concatenate(parts, axis=1)
+    update = lax.dot_general(
+        attended,
+        weights[:, 3 * inner :],
+        (((1,), (1,)), ((), ())),
+        preferred_element_type=jnp.float32,
+    )
+    return (stream.astype(jnp.float32) + update).astype(jnp.bfloat16)
+
+
+def row_mask(tokens, rows, cols):
+    def row_of(dim):
+        at = lax.broadcasted_iota(jnp.int32, (tokens, tokens), dim)
+        return lax.rem(lax.div(at, cols), rows)
+
+    return row_of(0) == row_of(1)
+
+
+def rows_kernel(inner, rows, cols, x_ref, g1_ref, w1_ref, g2_ref, w2_ref, o_ref):
+    stream = x_ref[...]
+    mask = row_mask(stream.shape[0], rows, cols)
+    stream = row_layer(stream, g1_ref[...], w1_ref[...], inner, mask)
+    o_ref[...] = row_layer(stream, g2_ref[...], w2_ref[...], inner, mask)
+
+
+def gathered_weights(qkv, out):
+    joined = jnp.concatenate([qkv, out.T], axis=1)
+    shares = lax.axis_size("batch") * lax.axis_size("view")
+    count = joined.shape[0] // shares
+    index = lax.axis_index("batch") * lax.axis_size("view") + lax.axis_index("view")
+    share = lax.dynamic_slice_in_dim(joined, index * count, count, axis=0)
+    return lax.all_gather(share, ("band", "batch", "view"), axis=0, tiled=True)
+
+
+def frame_sublayer(stream, gain, qkv, out):
+    inner = out.shape[0]
+    heads = inner // HEAD_DIM
+    tokens = stream.shape[0]
+    normed = rms_normed(stream, gain)
+    queries = (
+        jnp.dot(normed, qkv[:, :inner], preferred_element_type=jnp.float32)
+        .astype(jnp.bfloat16)
+        .reshape(tokens, heads, HEAD_DIM)
+    )
+    piece = lax.all_gather(normed, "band", axis=0, tiled=True)
+    count = piece.shape[0]
+    paired = jnp.dot(piece, qkv[:, inner:], preferred_element_type=jnp.float32).astype(jnp.bfloat16)
+    _, total, accum = online_update(
+        (jnp.full((heads, tokens), -1e30, jnp.float32), None, None),
+        queries,
+        paired[:, :inner].reshape(count, heads, HEAD_DIM),
+        paired[:, inner:].reshape(count, heads, HEAD_DIM),
+    )
+    attended = (accum / jnp.transpose(total)[:, :, None]).astype(jnp.bfloat16)
+    update = jnp.dot(attended.reshape(tokens, inner), out, preferred_element_type=jnp.float32)
+    return (stream.astype(jnp.float32) + update).astype(jnp.bfloat16)
+
+
+def local_swapped(
+    images,
+    frame_gain,
+    frame_qkv,
+    frame_out,
+    row1_gain,
+    row1_qkv,
+    row1_out,
+    row2_gain,
+    row2_qkv,
+    row2_out,
+):
+    _, row_count, col_count, width = images.shape
+    inner = frame_out.shape[0]
+    tokens = row_count * col_count
+    views = lax.axis_size("view")
+    first = gathered_weights(row1_qkv, row1_out)
+    second = gathered_weights(row2_qkv, row2_out)
+    stream = frame_sublayer(images.reshape(tokens, width), frame_gain, frame_qkv, frame_out)
+    swapped = lax.all_to_all(stream, "view", split_axis=0, concat_axis=0, tiled=True)
+    refined = pl.pallas_call(
+        functools.partial(rows_kernel, inner, row_count // views, col_count),
+        out_shape=jax.ShapeDtypeStruct((tokens, width), jnp.bfloat16),
+        compiler_params=pltpu.CompilerParams(vmem_limit_bytes=48 * 1024 * 1024),
+    )(swapped, row1_gain[None], first, row2_gain[None], second)
+    back = lax.all_to_all(refined, "view", split_axis=0, concat_axis=0, tiled=True)
+    return back.reshape(images.shape)
 
 
 def local(
@@ -190,4 +316,18 @@
         P(None, "band"),
     )
     out_specs = P(("batch", "view"), "band", None, None)
-    return jax.shard_map(local, mesh=mesh, in_specs=in_specs, out_specs=out_specs, check_vma=False)
+
+    def chosen(*arrays):
+        views, shares = mesh.shape["view"], mesh.shape["view"] * mesh.shape["batch"]
+        rows = arrays[0].shape[1] // mesh.shape["band"]
+        depth = arrays[5].shape[0] // mesh.shape["band"]
+        fits = rows % views == 0 and depth % (8 * shares) == 0
+        body = local_swapped if fits else local
+        return mapped(body)(*arrays)
+
+    def mapped(body):
+        return jax.shard_map(
+            body, mesh=mesh, in_specs=in_specs, out_specs=out_specs, check_vma=False
+        )
+
+    return chosen

time: 228 us -> 158 us (0.69)
  blocking collectives: 100 us -> 29.8 us
  waiting for transfers between devices: 46.6 us -> 92.7 us
  local copies, waits for them, and re-layouts: 24.8 us -> 3.3 us
  matrix products: 21.6 us -> 4.55 us
  starting transfers between devices: 14.3 us -> 3.51 us
  Pallas kernels: 0 us -> 6.61 us
    all_gather x2, waiting for transfers between devices: 37.2 us -> 87.9 us  [gathered_weights(): return lax.all_gather(share, ('band', 'batch', 'view'), axis=0, tiled=True)]
    all_gather x3 -> x1, blocking collectives: 72.6 us -> 22.3 us  [frame_sublayer(): piece = lax.all_gather(normed, 'band', axis=0, tiled=True)]
    all_to_all x4 -> x1, blocking collectives: 27.5 us -> 7.56 us  [local_swapped(): lax.all_to_all(refined, 'view', split_axis=0, concat_axis=0, tiled=True)]
    dot_general x71 -> x3, matrix products: 20.4 us -> 3.36 us  [the longest x1 1.41 us: frame_sublayer(): jnp.dot(normed, qkv[:, :inner], preferred_element_type=jnp.float32)]
    all_to_all x4 -> x1, starting transfers between devices: 14.3 us -> 3.43 us  [local_swapped(): lax.all_to_all(stream, 'view', split_axis=0, concat_axis=0, tiled=True)]
    all_gather x4 -> x0, local copies, waits for them, and re-layouts: 7.1 us -> none  [the longest x2 5.67 us: project_parts(): piece = lax.all_gather(shard, 'band', axis=0, tiled=True)]
    pallas_call x0 -> x1, Pallas kernels: none -> 6.61 us  [local_swapped(): pl.pallas_call(functools.partial(rows_kernel, inner, row_count // views,...]
    reshape x64 -> x0, local copies, waits for them, and re-layouts: 5.25 us -> none  [the longest x32 2.66 us: unit_attention(): keys = keys.reshape(length, 2, HEAD_DIM)]
  transfers between devices with their start and end apart: 6 -> 3, of which waited for: 4 -> 3; matrix products, arithmetic and copies ran while one was open for 12% -> 5% of each run, Pallas kernels for 0% -> 0%
where the time goes in v1:
time: 158 us
  waiting for transfers between devices  92.7 us (59%)
  blocking collectives  29.8 us (19%)
  between operations  13.5 us (9%)
  Pallas kernels  6.61 us (4%)
  matrix products  4.55 us (3%)
  other arithmetic  4.06 us (3%)
  starting transfers between devices  3.51 us (2%)
  local copies, waits for them, and re-layouts  3.3 us (2%)
    all_gather x2, waiting for transfers between devices, gathered_weights(): return lax.all_gather(share, ('band', 'batch', 'view'), axis=0, tiled=True)  87.9 us
    all_gather x1, blocking collectives, frame_sublayer(): piece = lax.all_gather(normed, 'band', axis=0, tiled=True)  22.3 us
    all_to_all x1, blocking collectives, local_swapped(): lax.all_to_all(refined, 'view', split_axis=0, concat_axis=0, tiled=True)  7.56 us
    pallas_call x1, Pallas kernels, local_swapped(): pl.pallas_call(functools.partial(rows_kernel, inner, row_count // views,...  6.61 us
    all_to_all x1, waiting for transfers between devices, local_swapped(): lax.all_to_all(stream, 'view', split_axis=0, concat_axis=0, tiled=True)  4.76 us
    all_to_all x1, starting transfers between devices, local_swapped(): lax.all_to_all(stream, 'view', split_axis=0, concat_axis=0, tiled=True)  3.43 us
    concatenate x2, other arithmetic, gathered_weights(): joined = jnp.concatenate([qkv, out.T], axis=1)  3.23 us
  transfers between devices with their start and end apart: 3, of which 3 were waited for; matrix products, arithmetic and copies ran while one was open for 5% of the time, Pallas kernels for 0%

profile of v1, /device:TPU:0, one launch (start us, length us, event | category | flops | bytes accessed | tf_op | source)
XLA Modules:
  0.0 158.1 jit_solution(10942376160014355991)
XLA Ops:
  6.5 0.0 copy-start
  6.5 0.0 copy-start.2
  6.5 0.0 copy-start.3
  6.5 0.0 copy-start.6
  6.5 0.0 all-gather.3.cloned.1.call-start
  6.6 1.7 %fusion.17 = bf16[24,2048]{1,0:T(8,128)(2,1)} fusion(s32[]{:T(128)S(6)} %select_n.4, bf16[192,1536]{1,0:T(8,128)(2,1)} %param.15, bf16[192,512]{1,0:T(8,128)(2,1)} %bitcast.38), kind=kLoop, calls=%fused_computation.25 | loop fusion | flops 196608 | bytes 884740 | tf_op jit(solution)/shard_map/concatenate | solution.py:180
  8.3 0.0 all-gather.3.cloned.1.call-update
  8.3 0.0 all-gather.5.cloned.1.call-start
  8.4 1.5 fusion.16
  9.9 0.0 all-gather.5.cloned.1.call-update
  9.9 0.0 copy-done.2
  9.9 0.1 multiply_reduce_fusion.1
  10.1 0.1 rsqrt.12
  10.1 0.0 copy-done.3
  10.1 0.1 fusion.15
  10.3 22.3 %all_gather.9 = bf16[512,768]{1,0:T(8,128)(2,1)S(1)} all-gather(bf16[128,768]{1,0:T(8,128)(2,1)S(1)} %fusion.15), channel_id=1, replica_groups=mesh['view'=2,'band'=4,'batch'=4] {'band'}, dimensions={0}, use_global_device_ids=true | all-gather | bytes 983040 | tf_op jit(solution)/shard_map/all_gather | solution.py:198
  32.6 0.0 copy-done.6
  32.6 1.0 fusion.4
  33.5 0.1 fusion.19
  33.6 0.2 copy.16
  33.8 1.4 convolution_convert_fusion
  35.3 0.1 copy.15
  35.4 0.2 copy.14
  35.6 0.6 multiply_reduce_fusion
  36.2 0.6 fusion
  36.7 0.0 copy-start.4
  36.8 0.0 copy-start.5
  36.8 0.6 fusion.9
  37.4 0.0 copy-done
  37.4 1.0 fusion.7
  38.4 3.4 %all-to-all-start = ((bf16[2,64,768]{2,1,0:T(8,128)(2,1)}), bf16[2,64,768]{2,1,0:T(8,128)(2,1)S(1)}, u32[]{:S(2)}, u32[]{:S(2)}) async-start(bf16[2,64,768]{2,1,0:T(8,128)(2,1)} %bitcast.7), calls=%async_computation | async-start | bytes 393216 | tf_op jit(solution)/shard_map/all_to_all | solution.py:231
  41.8 0.0 copy-done.4
  41.9 0.0 copy-done.5
  41.9 4.8 %all-to-all-done = bf16[2,64,768]{2,1,0:T(8,128)(2,1)S(1)} async-done(((bf16[2,64,768]{2,1,0:T(8,128)(2,1)}), bf16[2,64,768]{2,1,0:T(8,128)(2,1)S(1)}, u32[]{:S(2)}, u32[]{:S(2)}) %all-to-all-start) | async-done | bytes 196640 | tf_op jit(solution)/shard_map/all_to_all | solution.py:231
  46.6 27.1 %all-gather.3.cloned.1.call-done.w1_ref = bf16[768,2048]{1,0:T(8,128)(2,1)} async-done(((bf16[24,2048]{1,0:T(8,128)(2,1)}), bf16[768,2048]{1,0:T(8,128)(2,1)}) %all-gather.3.cloned.1.call-update) | async-done | bytes 3145744 | tf_op jit(solution)/shard_map/all_gather | solution.py:185
  73.7 60.8 %all-gather.5.cloned.1.call-done.w2_ref = bf16[768,2048]{1,0:T(8,128)(2,1)} async-done(((bf16[24,2048]{1,0:T(8,128)(2,1)}), bf16[768,2048]{1,0:T(8,128)(2,1)}) %all-gather.5.cloned.1.call-update) | async-done | bytes 3145744 | tf_op jit(solution)/shard_map/all_gather | solution.py:185
  134.5 0.0 copy-start.1
  134.5 1.9 %copy-done.1 = bf16[768,2048]{1,0:T(8,128)(2,1)S(1)} copy-done((bf16[768,2048]{1,0:T(8,128)(2,1)S(1)}, bf16[768,2048]{1,0:T(8,128)(2,1)}, u32[]{:S(2)}) %copy-start.1) | copy-done | bytes 3145752
  136.4 6.6 %shard_map.100 = bf16[128,768]{1,0:T(8,128)(2,1)S(1)} custom-call(bf16[128,768]{1,0:T(8,128)(2,1)S(1)} %bitcast.31, f32[1,768]{1,0:T(1,128)S(1)} %broadcast_in_dim.14.g1_ref, bf16[768,2048]{1,0:T(8,128)(2,1)S(1)} %copy-done.1, f32[1,768]{1,0:T(1,128)S(1)} %broadcast_in_dim.15.g2_ref, bf16[768,2048]{1,0:T(8,128)(2,1)} %all-gather.5.cloned.1.call-done.w2_ref), custom_call_target="tpu_custom_call" | custom-call | tf_op jit(solution)/shard_map/pallas_call | solution.py:232
  143.0 7.6 %all_to_all.20 = bf16[2,64,768]{2,1,0:T(8,128)(2,1)S(1)} all-to-all(bf16[2,64,768]{2,1,0:T(8,128)(2,1)S(1)} %bitcast.32), channel_id=1, replica_groups=mesh['view'=2,'band'=4,'batch'=4] {'view'}, dimensions={0} | all-to-all | bytes 393216 | tf_op jit(solution)/shard_map/all_to_all | solution.py:237
  150.6 0.7 copy.18
  (4 shorter events, 0.0 us)
Async XLA Ops:
  6.5 30.9 %copy-start = (bf16[512,768]{1,0:T(8,128)(2,1)S(1)}, bf16[512,768]{1,0:T(8,128)(2,1)}, u32[]{:S(2)}) copy-start(bf16[512,768]{1,0:T(8,128)(2,1)} %param.13) | copy-start | bytes 2359300
  6.5 3.4 %copy-start.2 = (bf16[1,8,16,768]{3,2,1,0:T(8,128)(2,1)S(1)}, bf16[1,8,16,768]{3,2,1,0:T(8,128)(2,1)}, u32[]{:S(2)}) copy-start(bf16[1,8,16,768]{3,2,1,0:T(8,128)(2,1)} %param.10) | copy-start | bytes 589828
  6.5 3.6 %copy-start.3 = (f32[768]{0:T(1024)S(1)}, f32[768]{0:T(1024)}, u32[]{:S(2)}) copy-start(f32[768]{0:T(1024)} %param.11) | copy-start | bytes 9220
  6.5 26.0 %copy-start.6 = (bf16[768,1536]{1,0:T(8,128)(2,1)S(1)}, bf16[768,1536]{1,0:T(8,128)(2,1)}, u32[]{:S(2)}) copy-start(bf16[768,1536]{1,0:T(8,128)(2,1)} %param.12) | copy-start | bytes 7077892
  6.5 67.2 %all-gather.3.cloned.1.call-start = ((), (), s32[]{:S(2)}) async-start(), calls=%async_computation.2 | async-start | bytes 3244032 | tf_op jit(solution)/shard_map/all_gather | solution.py:185
  8.3 126.2 %all-gather.5.cloned.1.call-start = ((), (), s32[]{:S(2)}) async-start(), calls=%async_computation.3 | async-start | bytes 3244032 | tf_op jit(solution)/shard_map/all_gather | solution.py:185
  36.7 5.1 %copy-start.4 = (f32[768]{0:T(1024)S(1)}, f32[768]{0:T(1024)}, u32[]{:S(2)}) copy-start(f32[768]{0:T(1024)} %param.14) | copy-start | bytes 9220
  36.8 5.1 %copy-start.5 = (f32[768]{0:T(1024)S(1)}, f32[768]{0:T(1024)}, u32[]{:S(2)}) copy-start(f32[768]{0:T(1024)} %param.17) | copy-start | bytes 9220
  38.4 8.2 %all-to-all-start = ((bf16[2,64,768]{2,1,0:T(8,128)(2,1)}), bf16[2,64,768]{2,1,0:T(8,128)(2,1)S(1)}, u32[]{:S(2)}, u32[]{:S(2)}) async-start(bf16[2,64,768]{2,1,0:T(8,128)(2,1)} %bitcast.7), calls=%async_computation | async-start | bytes 393216 | tf_op jit(solution)/shard_map/all_to_all | solution.py:231
  134.5 1.9 %copy-start.1 = (bf16[768,2048]{1,0:T(8,128)(2,1)S(1)}, bf16[768,2048]{1,0:T(8,128)(2,1)}, u32[]{:S(2)}) copy-start(bf16[768,2048]{1,0:T(8,128)(2,1)} %all-gather.3.cloned.1.call-done.w1_ref) | copy-start | bytes 9437188
Sparse Core Ops, SparseCore 0:
  10.3 63.3 all-gather.2
  76.6 57.8 all-gather.4

commit v2 on v1

--- a/solution.py
+++ b/solution.py
@@ -169,47 +169,252 @@
     return row_of(0) == row_of(1)
 
 
-def rows_kernel(inner, rows, cols, x_ref, g1_ref, w1_ref, g2_ref, w2_ref, o_ref):
-    stream = x_ref[...]
-    mask = row_mask(stream.shape[0], rows, cols)
-    stream = row_layer(stream, g1_ref[...], w1_ref[...], inner, mask)
-    o_ref[...] = row_layer(stream, g2_ref[...], w2_ref[...], inner, mask)
-
-
-def gathered_weights(qkv, out):
-    joined = jnp.concatenate([qkv, out.T], axis=1)
-    shares = lax.axis_size("batch") * lax.axis_size("view")
-    count = joined.shape[0] // shares
-    index = lax.axis_index("batch") * lax.axis_size("view") + lax.axis_index("view")
-    share = lax.dynamic_slice_in_dim(joined, index * count, count, axis=0)
-    return lax.all_gather(share, ("band", "batch", "view"), axis=0, tiled=True)
-
-
-def frame_sublayer(stream, gain, qkv, out):
-    inner = out.shape[0]
-    heads = inner // HEAD_DIM
-    tokens = stream.shape[0]
-    normed = rms_normed(stream, gain)
-    queries = (
-        jnp.dot(normed, qkv[:, :inner], preferred_element_type=jnp.float32)
-        .astype(jnp.bfloat16)
-        .reshape(tokens, heads, HEAD_DIM)
-    )
-    piece = lax.all_gather(normed, "band", axis=0, tiled=True)
-    count = piece.shape[0]
-    paired = jnp.dot(piece, qkv[:, inner:], preferred_element_type=jnp.float32).astype(jnp.bfloat16)
-    _, total, accum = online_update(
-        (jnp.full((heads, tokens), -1e30, jnp.float32), None, None),
-        queries,
-        paired[:, :inner].reshape(count, heads, HEAD_DIM),
-        paired[:, inner:].reshape(count, heads, HEAD_DIM),
-    )
-    attended = (accum / jnp.transpose(total)[:, :, None]).astype(jnp.bfloat16)
-    update = jnp.dot(attended.reshape(tokens, inner), out, preferred_element_type=jnp.float32)
-    return (stream.astype(jnp.float32) + update).astype(jnp.bfloat16)
+def kernel(
+    sizes,
+    rows,
+    cols,
+    x_ref,
+    frame_gain_ref,
+    frame_qkv_ref,
+    frame_out_ref,
+    gain1_ref,
+    part1_ref,
+    gain2_ref,
+    part2_ref,
+    o_ref,
+    whole,
+    sent,
+    got,
+    mixed,
+    returned,
+    stream_ref,
+    swapped,
+    refined,
+    back,
+    part_sem,
+    spread_send,
+    spread_recv,
+    hop_send,
+    hop_recv,
+    trio_send,
+    trio_recv,
+    mix_send,
+    mix_recv,
+    swap_send,
+    swap_recv,
+    back_send,
+    back_recv,
+):
+    views, bands, batches = sizes["view"], sizes["band"], sizes["batch"]
+    view, band, batch = lax.axis_index("view"), lax.axis_index("band"), lax.axis_index("batch")
+    tokens = x_ref.shape[0]
+    inner = frame_out_ref.shape[0]
+    pair = inner // bands
+    depth = part1_ref.shape[0]
+    share = part1_ref.shape[1] // (views * batches)
+    chunk = tokens // views
+
+    hops = []
+    for axis, at, size in (("view", view, views), ("batch", batch, batches)):
+        step = size // 2
+        while step:
+            bit = lax.rem(lax.div(at, step), 2)
+            hops.append((axis, at + step * (1 - 2 * bit), bit))
+            step //= 2
+    index = 0
+    for level, (_, _, bit) in enumerate(hops):
+        index = index + bit * 2**level
+
+    def ahead(d):
+        return lax.rem(band + d, bands)
+
+    def behind(d):
+        return lax.rem(band + bands - d, bands)
+
+    def other(d):
+        return lax.rem(view + d, views)
+
+    def remote(src, dst, send, recv, axis, to):
+        return pltpu.make_async_remote_copy(
+            src_ref=src,
+            dst_ref=dst,
+            send_sem=send,
+            recv_sem=recv,
+            device_id={axis: to},
+            device_id_type=pl.DeviceIdType.MESH,
+        )
+
+    def spread(layer, d):
+        columns = pl.ds(pl.multiple_of(index * share, share), share)
+        part = part1_ref if layer == 0 else part2_ref
+        at = pl.ds(pl.multiple_of(band * depth, depth), depth)
+        return remote(
+            part.at[:, columns],
+            whole.at[layer, at, columns],
+            spread_send.at[layer, d - 1],
+            spread_recv.at[layer, d - 1],
+            "band",
+            ahead(d),
+        )
+
+    def hop(layer, level, d):
+        axis, to, _ = hops[level]
+        held = share * 2**level
+        columns = pl.ds(pl.multiple_of(lax.div(index, 2**level) * held, held), held)
+        at = pl.ds(pl.multiple_of(behind(d) * depth, depth), depth)
+        block = whole.at[layer, at, columns]
+        return remote(
+            block,
+            block,
+            hop_send.at[layer, level, d - 1],
+            hop_recv.at[layer, level, d - 1],
+            axis,
+            to,
+        )
+
+    def trio(d):
+        return remote(
+            sent.at[ahead(d)], got.at[band], trio_send.at[d - 1], trio_recv.at[d - 1], "band", ahead(d)
+        )
+
+    def mix(d):
+        return remote(
+            mixed.at[ahead(d)],
+            returned.at[band],
+            mix_send.at[d - 1],
+            mix_recv.at[d - 1],
+            "band",
+            ahead(d),
+        )
+
+    def rows_of(at):
+        return pl.ds(pl.multiple_of(at * chunk, chunk), chunk)
+
+    def swap(src, dst, send, recv, d):
+        return remote(
+            src.at[rows_of(other(d))],
+            dst.at[rows_of(view)],
+            send.at[d - 1],
+            recv.at[d - 1],
+            "view",
+            other(d),
+        )
+
+    def pass_on(layer, level):
+        for d in range(1, bands):
+            if level == 0:
+                spread(layer, d).wait_recv()
+            else:
+                hop(layer, level - 1, d).wait_recv()
+            if level < len(hops):
+                hop(layer, level, d).start()
+
+    barrier = pltpu.get_barrier_semaphore()
+    greeted = 0
+    for axis, at, size in (("band", band, bands), ("view", view, views)):
+        for d in range(1, size):
+            pl.semaphore_signal(
+                barrier,
+                inc=1,
+                device_id={axis: lax.rem(at + d, size)},
+                device_id_type=pl.DeviceIdType.MESH,
+            )
+            greeted += 1
+    for axis, to, _ in hops:
+        if axis == "batch":
+            pl.semaphore_signal(
+                barrier, inc=1, device_id={axis: to}, device_id_type=pl.DeviceIdType.MESH
+            )
+            greeted += 1
+    own = pl.ds(pl.multiple_of(band * depth, depth), depth)
+    own_parts = [
+        pltpu.make_async_copy(part, whole.at[layer, own], part_sem.at[layer])
+        for layer, part in enumerate((part1_ref, part2_ref))
+    ]
+    for copy in own_parts:
+        copy.start()
+    normed = rms_normed(x_ref[...], frame_gain_ref[...])
+    projected = jnp.dot(normed, frame_qkv_ref[...], preferred_element_type=jnp.float32)
+    projected = projected.astype(jnp.bfloat16)
+    for t in range(bands):
+        for which in range(3):
+            at = which * inner + t * pair
+            sent[t, :, which * pair : (which + 1) * pair] = projected[:, at : at + pair]
+    pl.semaphore_wait(barrier, greeted)
+
+    for d in range(1, bands):
+        spread(0, d).start()
+    for d in range(1, bands):
+        trio(d).start()
+    for d in range(1, bands):
+        spread(1, d).start()
+    got[band] = sent[band]
+    pass_on(0, 0)
+    pass_on(0, 1)
+
+    for d in range(1, bands):
+        trio(d).wait_recv()
+    everyone = got[...].reshape(bands * tokens, 3 * pair)
+
+    def attend(at):
+        queries = got[at]
+        parts = []
+        for lo in range(0, pair, 2 * HEAD_DIM):
+            hi = lo + 2 * HEAD_DIM
+            parts.append(
+                attend_pair(
+                    queries[:, lo:hi],
+                    everyone[:, pair + lo : pair + hi],
+                    everyone[:, 2 * pair + lo : 2 * pair + hi],
+                    None,
+                )
+            )
+        return jnp.concatenate(parts, axis=1) if len(parts) > 1 else parts[0]
+
+    for d in range(1, bands):
+        mixed[ahead(d)] = attend(ahead(d))
+        mix(d).start()
+    returned[band] = attend(band)
+    for level in range(2, len(hops)):
+        pass_on(0, level)
+    pass_on(1, 0)
+    for d in range(1, bands):
+        mix(d).wait_recv()
+    attended = jnp.concatenate([returned[t] for t in range(bands)], axis=1)
+    update = jnp.dot(attended, frame_out_ref[...], preferred_element_type=jnp.float32)
+    stream_ref[...] = (x_ref[...].astype(jnp.float32) + update).astype(jnp.bfloat16)
+    for d in range(1, views):
+        swap(stream_ref, swapped, swap_send, swap_recv, d).start()
+    swapped[rows_of(view)] = stream_ref[rows_of(view)]
+    pass_on(1, 1)
+    for d in range(1, views):
+        swap(stream_ref, swapped, swap_send, swap_recv, d).wait_recv()
+    for copy in own_parts:
+        copy.wait()
+    pass_on(0, len(hops))
+    mask = row_mask(tokens, rows, cols)
+    stream = row_layer(swapped[...], gain1_ref[...], whole.at[0], inner, mask)
+    for level in range(2, len(hops) + 1):
+        pass_on(1, level)
+    refined[...] = row_layer(stream, gain2_ref[...], whole.at[1], inner, mask)
+    for d in range(1, views):
+        swap(refined, back, back_send, back_recv, d).start()
+    back[rows_of(view)] = refined[rows_of(view)]
+    for d in range(1, bands):
+        for layer in range(2):
+            spread(layer, d).wait_send()
+            for level in range(len(hops)):
+                hop(layer, level, d).wait_send()
+        trio(d).wait_send()
+        mix(d).wait_send()
+    for d in range(1, views):
+        swap(stream_ref, swapped, swap_send, swap_recv, d).wait_send()
+        swap(refined, back, back_send, back_recv, d).wait()
+    o_ref[...] = back[...]
 
 
 def local_swapped(
+    sizes,
     images,
     frame_gain,
     frame_qkv,
@@ -224,18 +429,58 @@
     _, row_count, col_count, width = images.shape
     inner = frame_out.shape[0]
     tokens = row_count * col_count
-    views = lax.axis_size("view")
-    first = gathered_weights(row1_qkv, row1_out)
-    second = gathered_weights(row2_qkv, row2_out)
-    stream = frame_sublayer(images.reshape(tokens, width), frame_gain, frame_qkv, frame_out)
-    swapped = lax.all_to_all(stream, "view", split_axis=0, concat_axis=0, tiled=True)
+    views, bands, batches = sizes["view"], sizes["band"], sizes["batch"]
+    depth = row1_qkv.shape[0]
+    pair = inner // bands
+    hops = (views * batches).bit_length() - 1
+    vmem = pl.BlockSpec(memory_space=pltpu.VMEM)
+    part1 = jnp.concatenate([row1_qkv, row1_out.T], axis=1)
+    part2 = jnp.concatenate([row2_qkv, row2_out.T], axis=1)
+    kind = jnp.bfloat16
+    dma = pltpu.SemaphoreType.DMA
     refined = pl.pallas_call(
-        functools.partial(rows_kernel, inner, row_count // views, col_count),
-        out_shape=jax.ShapeDtypeStruct((tokens, width), jnp.bfloat16),
-        compiler_params=pltpu.CompilerParams(vmem_limit_bytes=48 * 1024 * 1024),
-    )(swapped, row1_gain[None], first, row2_gain[None], second)
-    back = lax.all_to_all(refined, "view", split_axis=0, concat_axis=0, tiled=True)
-    return back.reshape(images.shape)
+        functools.partial(kernel, sizes, row_count // views, col_count),
+        out_shape=jax.ShapeDtypeStruct((tokens, width), kind),
+        in_specs=[vmem] * 8,
+        out_specs=vmem,
+        scratch_shapes=[
+            pltpu.VMEM((2, bands * depth, 4 * inner), kind),
+            pltpu.VMEM((bands, tokens, 3 * pair), kind),
+            pltpu.VMEM((bands, tokens, 3 * pair), kind),
+            pltpu.VMEM((bands, tokens, pair), kind),
+            pltpu.VMEM((bands, tokens, pair), kind),
+            pltpu.VMEM((tokens, width), kind),
+            pltpu.VMEM((tokens, width), kind),
+            pltpu.VMEM((tokens, width), kind),
+            pltpu.VMEM((tokens, width), kind),
+            dma((2,)),
+            dma((2, bands - 1)),
+            dma((2, bands - 1)),
+            dma((2, hops, bands - 1)),
+            dma((2, hops, bands - 1)),
+            dma((bands - 1,)),
+            dma((bands - 1,)),
+            dma((bands - 1,)),
+            dma((bands - 1,)),
+            dma((views - 1,)),
+            dma((views - 1,)),
+            dma((views - 1,)),
+            dma((views - 1,)),
+        ],
+        compiler_params=pltpu.CompilerParams(
+            collective_id=0, has_side_effects=True, vmem_limit_bytes=48 * 1024 * 1024
+        ),
+    )(
+        images.reshape(tokens, width),
+        frame_gain[None],
+        frame_qkv,
+        frame_out,
+        row1_gain[None],
+        part1,
+        row2_gain[None],
+        part2,
+    )
+    return refined.reshape(images.shape)
 
 
 def local(
@@ -317,17 +562,31 @@
     )
     out_specs = P(("batch", "view"), "band", None, None)
 
+    sizes = {name: mesh.shape[name] for name in ("view", "band", "batch")}
+
+    def fits(images, frame_out, row_qkv):
+        views, bands, batches = sizes["view"], sizes["band"], sizes["batch"]
+        rows = images.shape[1] // bands
+        inner, width = frame_out.shape
+        depth = row_qkv.shape[0] // bands
+        if min(views, bands, batches) < 2 or rows % views:
+            return False
+        return (
+            views & (views - 1) == 0
+            and batches & (batches - 1) == 0
+            and images.shape[0] == views * batches
+            and rows * images.shape[2] // views % 16 == 0
+            and depth % 16 == 0
+            and width == row_qkv.shape[0]
+            and inner % (bands * 2 * HEAD_DIM) == 0
+            and 4 * inner % (128 * views * batches) == 0
+        )
+
     def chosen(*arrays):
-        views, shares = mesh.shape["view"], mesh.shape["view"] * mesh.shape["batch"]
-        rows = arrays[0].shape[1] // mesh.shape["band"]
-        depth = arrays[5].shape[0] // mesh.shape["band"]
-        fits = rows % views == 0 and depth % (8 * shares) == 0
-        body = local_swapped if fits else local
-        return mapped(body)(*arrays)
-
-    def mapped(body):
+        fit = fits(arrays[0], arrays[3], arrays[5])
+        body = functools.partial(local_swapped, sizes) if fit else local
         return jax.shard_map(
             body, mesh=mesh, in_specs=in_specs, out_specs=out_specs, check_vma=False
-        )
+        )(*arrays)
 
     return chosen

time: 158 us -> 61 us (0.39)
  waiting for transfers between devices: 92.7 us -> 0 us
  Pallas kernels: 6.61 us -> 54.3 us
  blocking collectives: 29.8 us -> 0 us
  between operations: 13.5 us -> 0.02 us
  matrix products: 4.55 us -> 0 us
  starting transfers between devices: 3.51 us -> 0 us
  other arithmetic: 4.06 us -> 1.67 us
    all_gather x2 -> x0, waiting for transfers between devices: 87.9 us -> none  [gathered_weights(): return lax.all_gather(share, ('band', 'batch', 'view'), axis=0, tiled=True)]
    pallas_call x1, Pallas kernels: 6.61 us -> 54.3 us  [local_swapped(): pl.pallas_call(functools.partial(kernel, sizes, row_count // views, col_c...]
    all_gather x1 -> x0, blocking collectives: 22.3 us -> none  [frame_sublayer(): piece = lax.all_gather(normed, 'band', axis=0, tiled=True)]
    all_to_all x1 -> x0, blocking collectives: 7.56 us -> none  [local_swapped(): lax.all_to_all(refined, 'view', split_axis=0, concat_axis=0, tiled=True)]
    all_to_all x1 -> x0, waiting for transfers between devices: 4.76 us -> none  [local_swapped(): lax.all_to_all(stream, 'view', split_axis=0, concat_axis=0, tiled=True)]
    dot_general x5 -> x0, matrix products: 4.55 us -> none  [the longest x1 1.41 us: frame_sublayer(): jnp.dot(normed, qkv[:, :inner], preferred_element_type=jnp.float32)]
    all_to_all x1 -> x0, starting transfers between devices: 3.43 us -> none  [local_swapped(): lax.all_to_all(stream, 'view', split_axis=0, concat_axis=0, tiled=True)]
    concatenate x2 -> x1, other arithmetic: 3.23 us -> 1.67 us  [local_swapped(): part1 = jnp.concatenate([row1_qkv, row1_out.T], axis=1)]
  transfers between devices with their start and end apart: 3 -> 0, of which waited for: 3 -> 0; matrix products, arithmetic and copies ran while one was open for 5% -> 0% of each run, Pallas kernels for 0% -> 0%
where the time goes in v2:
time: 61 us; the launch traced here: 60.3 us
  Pallas kernels  54.3 us (89%)
  local copies, waits for them, and re-layouts  4.34 us (7%)
  other arithmetic  1.67 us (3%)
    pallas_call x1, Pallas kernels, local_swapped(): pl.pallas_call(functools.partial(kernel, sizes, row_count // views, col_c...  54.3 us
    unnamed x7, local copies, waits for them, and re-layouts  2.28 us
    concatenate x1, other arithmetic, local_swapped(): part1 = jnp.concatenate([row1_qkv, row1_out.T], axis=1)  1.67 us

profile of v2, /device:TPU:0, one launch (start us, length us, event | category | flops | bytes accessed | tf_op | source)
XLA Modules:
  0.0 60.3 jit_solution(18195921065096043378)
XLA Ops:
  0.0 0.7 %broadcast_in_dim.9.frame_gain_ref = f32[1,768]{1,0:T(1,128)S(1)} reshape(f32[768]{0:T(1024)} %param.11) | data formatting | bytes 6144 | tf_op jit(solution)/shard_map/broadcast_in_dim | solution.py:475
  0.7 0.7 %broadcast_in_dim.10.gain1_ref = f32[1,768]{1,0:T(1,128)S(1)} reshape(f32[768]{0:T(1024)} %param.14) | data formatting | bytes 6144 | tf_op jit(solution)/shard_map/broadcast_in_dim | solution.py:478
  1.4 0.7 %broadcast_in_dim.11.gain2_ref = f32[1,768]{1,0:T(1,128)S(1)} reshape(f32[768]{0:T(1024)} %param.17) | data formatting | bytes 6144 | tf_op jit(solution)/shard_map/broadcast_in_dim | solution.py:480
  2.1 0.0 copy-start
  2.1 0.0 copy-start.1
  2.1 1.7 %pad_maximum_fusion = (bf16[192,2048]{1,0:T(8,128)(2,1)S(1)}, bf16[192,2048]{1,0:T(8,128)(2,1)S(1)}) fusion(bf16[192,512]{1,0:T(8,128)(2,1)} %bitcast.6, bf16[192,1536]{1,0:T(8,128)(2,1)} %param.15, bf16[192,512]{1,0:T(8,128)(2,1)} %bitcast.7, bf16[192,1536]{1,0:T(8,128)(2,1)} %param.18), kind=kLoop, calls=%fused_computation | loop fusion | flops 3145728 | bytes 3145728 | tf_op jit(solution)/shard_map/concatenate | solution.py:437
  3.7 0.5 copy-done
  4.2 0.2 copy-done.1
  4.4 0.0 copy-start.2
  4.4 0.9 %copy-done.2 = bf16[1,8,16,768]{3,2,1,0:T(8,128)(2,1)S(1)} copy-done((bf16[1,8,16,768]{3,2,1,0:T(8,128)(2,1)S(1)}, bf16[1,8,16,768]{3,2,1,0:T(8,128)(2,1)}, u32[]{:S(2)}) %copy-start.2) | copy-done | bytes 196632
  5.3 54.3 %shard_map.100 = bf16[128,768]{1,0:T(8,128)(2,1)S(1)} custom-call(bf16[128,768]{1,0:T(8,128)(2,1)S(1)} %bitcast.5, f32[1,768]{1,0:T(1,128)S(1)} %broadcast_in_dim.9.frame_gain_ref, bf16[768,1536]{1,0:T(8,128)(2,1)S(1)} %copy-done, bf16[512,768]{1,0:T(8,128)(2,1)S(1)} %copy-done.1, f32[1,768]{1,0:T(1,128)S(1)} %broadcast_in_dim.10.gain1_ref, ...), custom_call_target="tpu_custom_call" | custom-call | tf_op jit(solution)/shard_map/pallas_call | solution.py:441
  59.6 0.7 %copy.12 = bf16[1,8,16,768]{3,2,1,0:T(8,128)(2,1)} copy(bf16[1,8,16,768]{3,2,1,0:T(8,128)(2,1)S(1)} %bitcast.4) | data formatting | bytes 393216
Async XLA Ops:
  2.1 2.2 %copy-start = (bf16[768,1536]{1,0:T(8,128)(2,1)S(1)}, bf16[768,1536]{1,0:T(8,128)(2,1)}, u32[]{:S(2)}) copy-start(bf16[768,1536]{1,0:T(8,128)(2,1)} %frame_qkv_ref.1) | copy-start | bytes 7077892
  2.1 2.3 %copy-start.1 = (bf16[512,768]{1,0:T(8,128)(2,1)S(1)}, bf16[512,768]{1,0:T(8,128)(2,1)}, u32[]{:S(2)}) copy-start(bf16[512,768]{1,0:T(8,128)(2,1)} %frame_out_ref.1) | copy-start | bytes 2359300
  4.4 0.9 %copy-start.2 = (bf16[1,8,16,768]{3,2,1,0:T(8,128)(2,1)S(1)}, bf16[1,8,16,768]{3,2,1,0:T(8,128)(2,1)}, u32[]{:S(2)}) copy-start(bf16[1,8,16,768]{3,2,1,0:T(8,128)(2,1)} %param.10) | copy-start | bytes 589828

commit v3 on v2

--- a/solution.py
+++ b/solution.py
@@ -221,9 +221,14 @@
             bit = lax.rem(lax.div(at, step), 2)
             hops.append((axis, at + step * (1 - 2 * bit), bit))
             step //= 2
-    index = 0
-    for level, (_, _, bit) in enumerate(hops):
-        index = index + bit * 2**level
+    streams = [hops, hops[1::-1] + hops[2:]]
+    half = depth // len(streams)
+    indices = []
+    for order in streams:
+        index = 0
+        for level, (_, _, bit) in enumerate(order):
+            index = index + bit * 2**level
+        indices.append(index)
 
     def ahead(d):
         return lax.rem(band + d, bands)
@@ -244,30 +249,79 @@
             device_id_type=pl.DeviceIdType.MESH,
         )
 
-    def spread(layer, d):
-        columns = pl.ds(pl.multiple_of(index * share, share), share)
+    def share_at(layer, stream, k):
+        at = pl.ds(pl.multiple_of(behind(k) * depth + stream * half, half), half)
+        columns = pl.ds(pl.multiple_of(indices[stream] * share, share), share)
+        return whole.at[layer, at, columns]
+
+    def spread_own(layer, stream, toward):
         part = part1_ref if layer == 0 else part2_ref
-        at = pl.ds(pl.multiple_of(band * depth, depth), depth)
+        columns = pl.ds(pl.multiple_of(indices[stream] * share, share), share)
         return remote(
-            part.at[:, columns],
-            whole.at[layer, at, columns],
-            spread_send.at[layer, d - 1],
-            spread_recv.at[layer, d - 1],
+            part.at[stream * half : (stream + 1) * half, columns],
+            share_at(layer, stream, 0),
+            spread_send.at[layer, stream, 0 if toward == 1 else 1],
+            spread_recv.at[layer, stream, 0 if toward == 1 else bands - 2],
             "band",
-            ahead(d),
-        )
-
-    def hop(layer, level, d):
-        axis, to, _ = hops[level]
+            band + toward,
+        )
+
+    def spread_on(layer, stream, k, toward):
+        block = share_at(layer, stream, k)
+        return remote(
+            block,
+            block,
+            spread_send.at[layer, stream, 1 + k],
+            spread_recv.at[layer, stream, k if toward == 1 else k - 2],
+            "band",
+            band + toward,
+        )
+
+    def spread_arrived(layer, stream, k):
+        block = share_at(layer, stream, k)
+        remote(
+            block,
+            block,
+            spread_send.at[layer, stream, 0],
+            spread_recv.at[layer, stream, k - 1],
+            "band",
+            ahead(1),
+        ).wait_recv()
+
+    def own_sends(layer, act):
+        for stream in range(len(streams)):
+            for toward, there in ((1, band < bands - 1), (-1, band > 0)):
+
+                @pl.when(there)
+                def _():
+                    act(spread_own(layer, stream, toward))
+
+    def forwards(layer, stream, k, act):
+        @pl.when((k <= band) & (band < bands - 1))
+        def _():
+            act(spread_on(layer, stream, k, 1))
+
+        @pl.when((k > band) & (band > 0))
+        def _():
+            act(spread_on(layer, stream, k, -1))
+
+    def nearest(t):
+        middle = (t + 1) // 2 if t % 2 else bands - t // 2
+        return jnp.where(band == 0, bands - t, jnp.where(band == bands - 1, t, middle))
+
+    def hop(layer, stream, level, k):
+        axis, to, _ = streams[stream][level]
         held = share * 2**level
-        columns = pl.ds(pl.multiple_of(lax.div(index, 2**level) * held, held), held)
-        at = pl.ds(pl.multiple_of(behind(d) * depth, depth), depth)
+        at = pl.ds(pl.multiple_of(behind(k) * depth + stream * half, half), half)
+        columns = pl.ds(
+            pl.multiple_of(lax.div(indices[stream], 2**level) * held, held), held
+        )
         block = whole.at[layer, at, columns]
         return remote(
             block,
             block,
-            hop_send.at[layer, level, d - 1],
-            hop_recv.at[layer, level, d - 1],
+            hop_send.at[layer, stream, level, k - 1],
+            hop_recv.at[layer, stream, level, k - 1],
             axis,
             to,
         )
@@ -301,13 +355,16 @@
         )
 
     def pass_on(layer, level):
-        for d in range(1, bands):
-            if level == 0:
-                spread(layer, d).wait_recv()
-            else:
-                hop(layer, level - 1, d).wait_recv()
-            if level < len(hops):
-                hop(layer, level, d).start()
+        for t in range(1, bands):
+            k = nearest(t)
+            for stream in range(len(streams)):
+                if level == 0:
+                    spread_arrived(layer, stream, k)
+                    forwards(layer, stream, k, lambda copy: copy.start())
+                else:
+                    hop(layer, stream, level - 1, k).wait_recv()
+                if level < len(hops):
+                    hop(layer, stream, level, k).start()
 
     barrier = pltpu.get_barrier_semaphore()
     greeted = 0
@@ -334,20 +391,17 @@
     for copy in own_parts:
         copy.start()
     normed = rms_normed(x_ref[...], frame_gain_ref[...])
+    pl.semaphore_wait(barrier, greeted)
+    own_sends(0, lambda copy: copy.start())
     projected = jnp.dot(normed, frame_qkv_ref[...], preferred_element_type=jnp.float32)
     projected = projected.astype(jnp.bfloat16)
     for t in range(bands):
         for which in range(3):
             at = which * inner + t * pair
             sent[t, :, which * pair : (which + 1) * pair] = projected[:, at : at + pair]
-    pl.semaphore_wait(barrier, greeted)
-
-    for d in range(1, bands):
-        spread(0, d).start()
     for d in range(1, bands):
         trio(d).start()
-    for d in range(1, bands):
-        spread(1, d).start()
+    own_sends(1, lambda copy: copy.start())
     got[band] = sent[band]
     pass_on(0, 0)
     pass_on(0, 1)
@@ -400,11 +454,14 @@
     for d in range(1, views):
         swap(refined, back, back_send, back_recv, d).start()
     back[rows_of(view)] = refined[rows_of(view)]
+    for layer in range(2):
+        own_sends(layer, lambda copy: copy.wait_send())
     for d in range(1, bands):
         for layer in range(2):
-            spread(layer, d).wait_send()
-            for level in range(len(hops)):
-                hop(layer, level, d).wait_send()
+            for stream in range(len(streams)):
+                forwards(layer, stream, d, lambda copy: copy.wait_send())
+                for level in range(len(hops)):
+                    hop(layer, stream, level, d).wait_send()
         trio(d).wait_send()
         mix(d).wait_send()
     for d in range(1, views):
@@ -454,10 +511,10 @@
             pltpu.VMEM((tokens, width), kind),
             pltpu.VMEM((tokens, width), kind),
             dma((2,)),
-            dma((2, bands - 1)),
-            dma((2, bands - 1)),
-            dma((2, hops, bands - 1)),
-            dma((2, hops, bands - 1)),
+            dma((2, 2, bands + 1)),
+            dma((2, 2, bands - 1)),
+            dma((2, 2, hops, bands - 1)),
+            dma((2, 2, hops, bands - 1)),
             dma((bands - 1,)),
             dma((bands - 1,)),
             dma((bands - 1,)),
@@ -472,12 +529,12 @@
         ),
     )(
         images.reshape(tokens, width),
-        frame_gain[None],
+        frame_gain,
         frame_qkv,
         frame_out,
-        row1_gain[None],
+        row1_gain,
         part1,
-        row2_gain[None],
+        row2_gain,
         part2,
     )
     return refined.reshape(images.shape)
@@ -569,14 +626,14 @@
         rows = images.shape[1] // bands
         inner, width = frame_out.shape
         depth = row_qkv.shape[0] // bands
-        if min(views, bands, batches) < 2 or rows % views:
+        if min(views, bands, batches) < 2 or bands > 4 or rows % views:
             return False
         return (
             views & (views - 1) == 0
             and batches & (batches - 1) == 0
             and images.shape[0] == views * batches
             and rows * images.shape[2] // views % 16 == 0
-            and depth % 16 == 0
+            and depth % 32 == 0
             and width == row_qkv.shape[0]
             and inner % (bands * 2 * HEAD_DIM) == 0
             and 4 * inner % (128 * views * batches) == 0

time: 61 us -> 59 us (0.967)
  Pallas kernels: 54.3 us -> 52.2 us
    pallas_call x1, Pallas kernels: 54.3 us -> 52.2 us  [local_swapped(): pl.pallas_call(functools.partial(kernel, sizes, row_count // views, col_c...]
    broadcast_in_dim x3 -> x0, local copies, waits for them, and re-layouts: 2.07 us -> none  [the longest x1 0.69 us: local_swapped(): row2_gain[None]]
    unnamed x7 -> x13, local copies, waits for them, and re-layouts: 2.28 us -> 4.34 us
where the time goes in v3:
time: 59 us; the launch traced here: 58.2 us
  Pallas kernels  52.2 us (88%)
  local copies, waits for them, and re-layouts  4.34 us (7%)
  other arithmetic  1.67 us (3%)
    pallas_call x1, Pallas kernels, local_swapped(): pl.pallas_call(functools.partial(kernel, sizes, row_count // views, col_c...  52.2 us
    unnamed x13, local copies, waits for them, and re-layouts  4.34 us
    concatenate x1, other arithmetic, local_swapped(): part1 = jnp.concatenate([row1_qkv, row1_out.T], axis=1)  1.67 us

profile of v3, /device:TPU:0, one launch (start us, length us, event | category | flops | bytes accessed | tf_op | source)
XLA Modules:
  0.0 58.2 jit_solution(11335339682575419844)
XLA Ops:
  0.0 0.0 copy-start
  0.0 0.0 copy-start.1
  0.0 1.7 %pad_maximum_fusion = (bf16[192,2048]{1,0:T(8,128)(2,1)S(1)}, bf16[192,2048]{1,0:T(8,128)(2,1)S(1)}) fusion(bf16[192,512]{1,0:T(8,128)(2,1)} %bitcast.6, bf16[192,1536]{1,0:T(8,128)(2,1)} %param.15, bf16[192,512]{1,0:T(8,128)(2,1)} %bitcast.7, bf16[192,1536]{1,0:T(8,128)(2,1)} %param.18), kind=kLoop, calls=%fused_computation | loop fusion | flops 3145728 | bytes 3145728 | tf_op jit(solution)/shard_map/concatenate | solution.py:494
  1.7 0.5 copy-done
  2.2 0.2 copy-done.1
  2.4 0.0 copy-start.2
  2.4 0.9 %copy-done.2 = bf16[1,8,16,768]{3,2,1,0:T(8,128)(2,1)S(1)} copy-done((bf16[1,8,16,768]{3,2,1,0:T(8,128)(2,1)S(1)}, bf16[1,8,16,768]{3,2,1,0:T(8,128)(2,1)}, u32[]{:S(2)}) %copy-start.2) | copy-done | bytes 196632
  3.3 0.0 copy-start.3
  3.3 0.7 %copy-done.3 = f32[768]{0:T(1024)S(1)} copy-done((f32[768]{0:T(1024)S(1)}, f32[768]{0:T(1024)}, u32[]{:S(2)}) %copy-start.3) | copy-done | bytes 3096
  4.0 0.0 copy-start.4
  4.0 0.7 %copy-done.4 = f32[768]{0:T(1024)S(1)} copy-done((f32[768]{0:T(1024)S(1)}, f32[768]{0:T(1024)}, u32[]{:S(2)}) %copy-start.4) | copy-done | bytes 3096
  4.7 0.0 copy-start.5
  4.7 0.7 %copy-done.5 = f32[768]{0:T(1024)S(1)} copy-done((f32[768]{0:T(1024)S(1)}, f32[768]{0:T(1024)}, u32[]{:S(2)}) %copy-start.5) | copy-done | bytes 3096
  5.3 52.2 %shard_map.100 = bf16[128,768]{1,0:T(8,128)(2,1)S(1)} custom-call(bf16[128,768]{1,0:T(8,128)(2,1)S(1)} %bitcast.5, f32[768]{0:T(1024)S(1)} %copy-done.3, bf16[768,1536]{1,0:T(8,128)(2,1)S(1)} %copy-done, bf16[512,768]{1,0:T(8,128)(2,1)S(1)} %copy-done.1, f32[768]{0:T(1024)S(1)} %copy-done.4, bf16[192,2048]{1,0:T(8,128)(2,1)S(1)} %get-tuple-element.5.part1_ref, ...), custom_call_target="tpu_custom_call" | custom-call | tf_op jit(solution)/shard_map/pallas_call | solution.py:498
  57.5 0.7 %copy.12 = bf16[1,8,16,768]{3,2,1,0:T(8,128)(2,1)} copy(bf16[1,8,16,768]{3,2,1,0:T(8,128)(2,1)S(1)} %bitcast.4) | data formatting | bytes 393216
Async XLA Ops:
  0.0 2.2 %copy-start = (bf16[768,1536]{1,0:T(8,128)(2,1)S(1)}, bf16[768,1536]{1,0:T(8,128)(2,1)}, u32[]{:S(2)}) copy-start(bf16[768,1536]{1,0:T(8,128)(2,1)} %frame_qkv_ref.1) | copy-start | bytes 7077892
  0.0 2.3 %copy-start.1 = (bf16[512,768]{1,0:T(8,128)(2,1)S(1)}, bf16[512,768]{1,0:T(8,128)(2,1)}, u32[]{:S(2)}) copy-start(bf16[512,768]{1,0:T(8,128)(2,1)} %frame_out_ref.1) | copy-start | bytes 2359300
  2.4 0.9 %copy-start.2 = (bf16[1,8,16,768]{3,2,1,0:T(8,128)(2,1)S(1)}, bf16[1,8,16,768]{3,2,1,0:T(8,128)(2,1)}, u32[]{:S(2)}) copy-start(bf16[1,8,16,768]{3,2,1,0:T(8,128)(2,1)} %param.10) | copy-start | bytes 589828
  3.3 0.7 %copy-start.3 = (f32[768]{0:T(1024)S(1)}, f32[768]{0:T(1024)}, u32[]{:S(2)}) copy-start(f32[768]{0:T(1024)} %frame_gain_ref.1) | copy-start | bytes 9220
  4.0 0.7 %copy-start.4 = (f32[768]{0:T(1024)S(1)}, f32[768]{0:T(1024)}, u32[]{:S(2)}) copy-start(f32[768]{0:T(1024)} %gain1_ref.1) | copy-start | bytes 9220
  4.7 0.7 %copy-start.5 = (f32[768]{0:T(1024)S(1)}, f32[768]{0:T(1024)}, u32[]{:S(2)}) copy-start(f32[768]{0:T(1024)} %gain2_ref.1) | copy-start | bytes 9220

commit v4 on v3

--- a/solution.py
+++ b/solution.py
@@ -173,15 +173,25 @@
     sizes,
     rows,
     cols,
+    x_hbm,
+    frame_gain_hbm,
+    frame_qkv_hbm,
+    frame_out_hbm,
+    gain1_hbm,
+    qkv1_hbm,
+    out1_hbm,
+    gain2_hbm,
+    qkv2_hbm,
+    out2_hbm,
+    o_ref,
     x_ref,
     frame_gain_ref,
     frame_qkv_ref,
     frame_out_ref,
     gain1_ref,
-    part1_ref,
     gain2_ref,
-    part2_ref,
-    o_ref,
+    parts,
+    load_sem,
     whole,
     sent,
     got,
@@ -207,11 +217,11 @@
 ):
     views, bands, batches = sizes["view"], sizes["band"], sizes["batch"]
     view, band, batch = lax.axis_index("view"), lax.axis_index("band"), lax.axis_index("batch")
-    tokens = x_ref.shape[0]
-    inner = frame_out_ref.shape[0]
+    tokens = x_hbm.shape[0]
+    inner = frame_out_hbm.shape[0]
     pair = inner // bands
-    depth = part1_ref.shape[0]
-    share = part1_ref.shape[1] // (views * batches)
+    depth = qkv1_hbm.shape[0]
+    share = parts.shape[2] // (views * batches)
     chunk = tokens // views
 
     hops = []
@@ -255,10 +265,9 @@
         return whole.at[layer, at, columns]
 
     def spread_own(layer, stream, toward):
-        part = part1_ref if layer == 0 else part2_ref
         columns = pl.ds(pl.multiple_of(indices[stream] * share, share), share)
         return remote(
-            part.at[stream * half : (stream + 1) * half, columns],
+            parts.at[layer, stream * half : (stream + 1) * half, columns],
             share_at(layer, stream, 0),
             spread_send.at[layer, stream, 0 if toward == 1 else 1],
             spread_recv.at[layer, stream, 0 if toward == 1 else bands - 2],
@@ -365,6 +374,23 @@
                     hop(layer, stream, level - 1, k).wait_recv()
                 if level < len(hops):
                     hop(layer, stream, level, k).start()
+
+    loads = {}
+    for at, (name, src, dst) in enumerate(
+        (
+            ("out1", out1_hbm, parts.at[0, :, 3 * inner :]),
+            ("qkv1", qkv1_hbm, parts.at[0, :, : 3 * inner]),
+            ("x", x_hbm, x_ref),
+            ("frame_gain", frame_gain_hbm, frame_gain_ref),
+            ("frame_qkv", frame_qkv_hbm, frame_qkv_ref),
+            ("out2", out2_hbm, parts.at[1, :, 3 * inner :]),
+            ("qkv2", qkv2_hbm, parts.at[1, :, : 3 * inner]),
+            ("frame_out", frame_out_hbm, frame_out_ref),
+            ("gain1", gain1_hbm, gain1_ref),
+            ("gain2", gain2_hbm, gain2_ref),
+        )
+    ):
+        loads[name] = pltpu.make_async_copy(src, dst, load_sem.at[at])
 
     barrier = pltpu.get_barrier_semaphore()
     greeted = 0
@@ -384,15 +410,22 @@
             )
             greeted += 1
     own = pl.ds(pl.multiple_of(band * depth, depth), depth)
+    for copy in loads.values():
+        copy.start()
     own_parts = [
-        pltpu.make_async_copy(part, whole.at[layer, own], part_sem.at[layer])
-        for layer, part in enumerate((part1_ref, part2_ref))
+        pltpu.make_async_copy(parts.at[layer], whole.at[layer, own], part_sem.at[layer])
+        for layer in range(2)
     ]
-    for copy in own_parts:
-        copy.start()
-    normed = rms_normed(x_ref[...], frame_gain_ref[...])
+
+    loads["out1"].wait()
+    loads["qkv1"].wait()
     pl.semaphore_wait(barrier, greeted)
     own_sends(0, lambda copy: copy.start())
+    own_parts[0].start()
+    loads["x"].wait()
+    loads["frame_gain"].wait()
+    normed = rms_normed(x_ref[...], frame_gain_ref[...])
+    loads["frame_qkv"].wait()
     projected = jnp.dot(normed, frame_qkv_ref[...], preferred_element_type=jnp.float32)
     projected = projected.astype(jnp.bfloat16)
     for t in range(bands):
@@ -401,6 +434,9 @@
             sent[t, :, which * pair : (which + 1) * pair] = projected[:, at : at + pair]
     for d in range(1, bands):
         trio(d).start()
+    loads["out2"].wait()
+    loads["qkv2"].wait()
+    own_parts[1].start()
     own_sends(1, lambda copy: copy.start())
     got[band] = sent[band]
     pass_on(0, 0)
@@ -434,6 +470,8 @@
     pass_on(1, 0)
     for d in range(1, bands):
         mix(d).wait_recv()
+    for name in ("frame_out", "gain1", "gain2"):
+        loads[name].wait()
     attended = jnp.concatenate([returned[t] for t in range(bands)], axis=1)
     update = jnp.dot(attended, frame_out_ref[...], preferred_element_type=jnp.float32)
     stream_ref[...] = (x_ref[...].astype(jnp.float32) + update).astype(jnp.bfloat16)
@@ -491,16 +529,22 @@
     pair = inner // bands
     hops = (views * batches).bit_length() - 1
     vmem = pl.BlockSpec(memory_space=pltpu.VMEM)
-    part1 = jnp.concatenate([row1_qkv, row1_out.T], axis=1)
-    part2 = jnp.concatenate([row2_qkv, row2_out.T], axis=1)
     kind = jnp.bfloat16
     dma = pltpu.SemaphoreType.DMA
     refined = pl.pallas_call(
         functools.partial(kernel, sizes, row_count // views, col_count),
         out_shape=jax.ShapeDtypeStruct((tokens, width), kind),
-        in_specs=[vmem] * 8,
+        in_specs=[pl.BlockSpec(memory_space=pltpu.HBM)] * 10,
         out_specs=vmem,
         scratch_shapes=[
+            pltpu.VMEM((tokens, width), kind),
+            pltpu.VMEM(frame_gain.shape, frame_gain.dtype),
+            pltpu.VMEM(frame_qkv.shape, kind),
+            pltpu.VMEM(frame_out.shape, kind),
+            pltpu.VMEM(row1_gain.shape, row1_gain.dtype),
+            pltpu.VMEM(row2_gain.shape, row2_gain.dtype),
+            pltpu.VMEM((2, depth, 4 * inner), kind),
+            dma((10,)),
             pltpu.VMEM((2, bands * depth, 4 * inner), kind),
             pltpu.VMEM((bands, tokens, 3 * pair), kind),
             pltpu.VMEM((bands, tokens, 3 * pair), kind),
@@ -525,7 +569,7 @@
             dma((views - 1,)),
         ],
         compiler_params=pltpu.CompilerParams(
-            collective_id=0, has_side_effects=True, vmem_limit_bytes=48 * 1024 * 1024
+            collective_id=0, has_side_effects=True, vmem_limit_bytes=63 * 1024 * 1024
         ),
     )(
         images.reshape(tokens, width),
@@ -533,9 +577,11 @@
         frame_qkv,
         frame_out,
         row1_gain,
-        part1,
+        row1_qkv,
+        row1_out.T,
         row2_gain,
-        part2,
+        row2_qkv,
+        row2_out.T,
     )
     return refined.reshape(images.shape)
 

time: 59 us -> 55.4 us (0.939)
  local copies, waits for them, and re-layouts: 4.34 us -> 1.62 us
  other arithmetic: 1.67 us -> 0 us
  Pallas kernels: 52.2 us -> 53.4 us
    unnamed x13 -> x1, local copies, waits for them, and re-layouts: 4.34 us -> 1.62 us
    concatenate x1 -> x0, other arithmetic: 1.67 us -> none  [local_swapped(): part1 = jnp.concatenate([row1_qkv, row1_out.T], axis=1)]
    pallas_call x1, Pallas kernels: 52.2 us -> 53.4 us  [local_swapped(): pl.pallas_call(functools.partial(kernel, sizes, row_count // views, col_c...]
where the time goes in v4:
time: 55.4 us; the launch traced here: 55 us
  Pallas kernels  53.4 us (96%)
  local copies, waits for them, and re-layouts  1.62 us (3%)
    pallas_call x1, Pallas kernels, local_swapped(): pl.pallas_call(functools.partial(kernel, sizes, row_count // views, col_c...  53.4 us
    unnamed x1, local copies, waits for them, and re-layouts  1.62 us

profile of v4, /device:TPU:0, one launch (start us, length us, event | category | flops | bytes accessed | tf_op | source)
XLA Modules:
  0.0 55.0 jit_solution(5283061943799034692)
XLA Ops:
  0.0 53.4 %shard_map.100 = bf16[128,768]{1,0:T(8,128)(2,1)} custom-call(bf16[128,768]{1,0:T(8,128)(2,1)} %bitcast.5, f32[768]{0:T(1024)} %frame_gain_hbm.1, bf16[768,1536]{1,0:T(8,128)(2,1)} %frame_qkv_hbm.1, bf16[512,768]{1,0:T(8,128)(2,1)} %frame_out_hbm.1, f32[768]{0:T(1024)} %gain1_hbm.1, bf16[192,1536]{1,0:T(8,128)(2,1)} %qkv1_hbm.1, bf16[192,512]{1,0:T(8,128)(2,1)} %bitcast.6, ...), custom_call_target="tpu_custom_call" | custom-call | tf_op jit(solution)/shard_map/pallas_call | solution.py:534
  53.4 1.6 %copy.12 = bf16[1,8,16,768]{3,2,1,0:T(8,128)(2,1)} copy(bf16[1,8,16,768]{3,2,1,0:T(8,128)(2,1)} %bitcast.4) | data formatting | bytes 393216

commit v5 on v4

--- a/solution.py
+++ b/solution.py
@@ -465,9 +465,9 @@
         mixed[ahead(d)] = attend(ahead(d))
         mix(d).start()
     returned[band] = attend(band)
+    pass_on(1, 0)
     for level in range(2, len(hops)):
         pass_on(0, level)
-    pass_on(1, 0)
     for d in range(1, bands):
         mix(d).wait_recv()
     for name in ("frame_out", "gain1", "gain2"):

time: 55.4 us -> 53.2 us (0.960)
  Pallas kernels: 53.4 us -> 51 us
    pallas_call x1, Pallas kernels: 53.4 us -> 51 us  [local_swapped(): pl.pallas_call(functools.partial(kernel, sizes, row_count // views, col_c...]
where the time goes in v5:
time: 53.2 us; the launch traced here: 52.7 us
  Pallas kernels  51 us (96%)
  local copies, waits for them, and re-layouts  1.62 us (3%)
    pallas_call x1, Pallas kernels, local_swapped(): pl.pallas_call(functools.partial(kernel, sizes, row_count // views, col_c...  51 us
    unnamed x1, local copies, waits for them, and re-layouts  1.62 us

profile of v5, /device:TPU:0, one launch (start us, length us, event | category | flops | bytes accessed | tf_op | source)
XLA Modules:
  0.0 52.7 jit_solution(6961757708326085655)
XLA Ops:
  0.0 51.0 %shard_map.100 = bf16[128,768]{1,0:T(8,128)(2,1)} custom-call(bf16[128,768]{1,0:T(8,128)(2,1)} %bitcast.5, f32[768]{0:T(1024)} %frame_gain_hbm.1, bf16[768,1536]{1,0:T(8,128)(2,1)} %frame_qkv_hbm.1, bf16[512,768]{1,0:T(8,128)(2,1)} %frame_out_hbm.1, f32[768]{0:T(1024)} %gain1_hbm.1, bf16[192,1536]{1,0:T(8,128)(2,1)} %qkv1_hbm.1, bf16[192,512]{1,0:T(8,128)(2,1)} %bitcast.6, ...), custom_call_target="tpu_custom_call" | custom-call | tf_op jit(solution)/shard_map/pallas_call | solution.py:534
  51.1 1.6 %copy.12 = bf16[1,8,16,768]{3,2,1,0:T(8,128)(2,1)} copy(bf16[1,8,16,768]{3,2,1,0:T(8,128)(2,1)} %bitcast.4) | data formatting | bytes 393216

commit v6 on v5

--- a/solution.py
+++ b/solution.py
@@ -363,8 +363,8 @@
             other(d),
         )
 
-    def pass_on(layer, level):
-        for t in range(1, bands):
+    def pass_on(layer, level, turns=range(1, bands)):
+        for t in turns:
             k = nearest(t)
             for stream in range(len(streams)):
                 if level == 0:
@@ -464,8 +464,8 @@
     for d in range(1, bands):
         mixed[ahead(d)] = attend(ahead(d))
         mix(d).start()
+        pass_on(1, 0, (d,))
     returned[band] = attend(band)
-    pass_on(1, 0)
     for level in range(2, len(hops)):
         pass_on(0, level)
     for d in range(1, bands):

time: 53.2 us -> 52.9 us (level)
  no operation moved by 1% of the time
where the time goes in v6:
time: 52.9 us; the launch traced here: 52.4 us
  Pallas kernels  50.8 us (96%)
  local copies, waits for them, and re-layouts  1.62 us (3%)
    pallas_call x1, Pallas kernels, local_swapped(): pl.pallas_call(functools.partial(kernel, sizes, row_count // views, col_c...  50.8 us
    unnamed x1, local copies, waits for them, and re-layouts  1.62 us

profile of v6, /device:TPU:0, one launch (start us, length us, event | category | flops | bytes accessed | tf_op | source)
XLA Modules:
  0.0 52.4 jit_solution(17199409782328695365)
XLA Ops:
  0.0 50.8 %shard_map.100 = bf16[128,768]{1,0:T(8,128)(2,1)} custom-call(bf16[128,768]{1,0:T(8,128)(2,1)} %bitcast.5, f32[768]{0:T(1024)} %frame_gain_hbm.1, bf16[768,1536]{1,0:T(8,128)(2,1)} %frame_qkv_hbm.1, bf16[512,768]{1,0:T(8,128)(2,1)} %frame_out_hbm.1, f32[768]{0:T(1024)} %gain1_hbm.1, bf16[192,1536]{1,0:T(8,128)(2,1)} %qkv1_hbm.1, bf16[192,512]{1,0:T(8,128)(2,1)} %bitcast.6, ...), custom_call_target="tpu_custom_call" | custom-call | tf_op jit(solution)/shard_map/pallas_call | solution.py:534
  50.8 1.6 %copy.12 = bf16[1,8,16,768]{3,2,1,0:T(8,128)(2,1)} copy(bf16[1,8,16,768]{3,2,1,0:T(8,128)(2,1)} %bitcast.4) | data formatting | bytes 393216
